TPU v7x, 256 devices: a whole 4x4x8 slice. The times are simulated.
256 devices in a mesh: pool: 16 (over x, y), head: 16 (over z, core).
Axes of the slice: x: 4, y: 4, z: 8, core: 2. Of those that a mesh axis runs over, the one named last changes fastest.
Arguments:
- q_nope: bfloat16 [4096, 16384], P('pool', 'head'), may hold values from -6 to 6
- q_rope: bfloat16 [4096, 8192], P('pool', 'head'), may hold values from -8 to 8
- new_latent: bfloat16 [4096, 512], P('pool'), may hold values from -6 to 6
- new_rope: bfloat16 [64, 4096], P(None, 'pool'), may hold values from -8 to 8
- resident_latent: bfloat16 [16, 256, 512], P('pool'), may hold values from -6 to 6
- resident_rope: bfloat16 [16, 64, 256], P('pool'), may hold values from -6 to 6
- pool_latent: bfloat16 [512, 64, 512], P('pool'), may hold values from -6 to 6
- pool_rope: bfloat16 [512, 4096], P('pool'), may hold values from -6 to 6
- block_table: int32 [16, 32], replicated, may hold values from -1 to 511, as said below
- resident_len: int32 [16], P('pool'), may hold values from 1 to 256, as said below
- suffix_len: int32 [16], P('pool'), may hold values from 128 to 256, as said below
- w_uk: bfloat16 [128, 128, 512], P('head'), may hold values from -0.5 to 0.5
- w_uv: bfloat16 [128, 512, 128], P('head'), may hold values from -0.25 to 0.25
- w_out: bfloat16 [16384, 3584], P('head'), may hold values from -0.375 to 0.375
Outputs:
- attn_out: bfloat16 [4096, 3584], P('pool', 'head')
Inputs may be any that keep to these rules, and one draw needn't show every extreme that they name: `block_table`: row s lists session s's restored blocks as pool device times 32 plus slot, in any order, then -1 entries; no block twice in the table; at most 2 blocks of one session lie on one pool device, every session has 2 on some pool device, and some session has 2 on every pool device. `resident_len`: some session has 256. `suffix_len`: some session has 256.
All inputs are finite; a program needn't handle non-finite values.
Results may differ from a plain program's by a relative error of at most 0.023.
Values may be sent and summed in bfloat16 or wider, within the bound.
A program may use at most 64 MiB of HBM per device.

v0:
```python
import jax
import jax.numpy as jnp
from jax import lax
from jax.sharding import PartitionSpec as P

NOPE = 128
ROPE = 64
KV = 512
VD = 128
BLK = 64
CAP = 2
SUF = 256
RES = 256


group_heads = 4


def attend_group(query_abs, query_rot, key_latent, key_rotary, valid, score_scale):
    scores = jnp.einsum("tgc,lc->tgl", query_abs, key_latent, preferred_element_type=jnp.float32)
    scores = scores + jnp.einsum(
        "tgr,rl->tgl", query_rot, key_rotary, preferred_element_type=jnp.float32
    )
    scores = jnp.where(valid[:, None, :], scores * score_scale, -jnp.inf)
    row_max = jnp.max(scores, axis=2, keepdims=True)
    exp_scores = jnp.exp(scores - row_max)
    denominator = jnp.sum(exp_scores, axis=2, keepdims=True)
    weights = exp_scores.astype(jnp.bfloat16)
    context = jnp.einsum("tgl,lc->tgc", weights, key_latent, preferred_element_type=jnp.float32)
    return (context / denominator).astype(jnp.bfloat16)


def body(
    q_nope,
    q_rope,
    new_latent,
    new_rope,
    resident_latent,
    resident_rope,
    pool_latent,
    pool_rope,
    block_table,
    resident_len,
    suffix_len,
    w_uk,
    w_uv,
    w_out,
):
    pool_count = lax.axis_size("pool")
    pool_index = lax.axis_index("pool")
    slot_count = pool_latent.shape[0]
    safe_ids = jnp.maximum(block_table, 0)
    source = jnp.where(block_table >= 0, safe_ids // slot_count, -1)
    owned_here = (source == pool_index).astype(jnp.int32)
    order_rank = jnp.cumsum(owned_here, axis=1) - owned_here
    block_rank = jnp.arange(CAP, dtype=jnp.int32)
    chosen = owned_here[:, None, :] * (order_rank[:, None, :] == block_rank[None, :, None]).astype(
        jnp.int32
    )
    local_slot = jnp.sum(chosen * (safe_ids % slot_count)[:, None, :], axis=2)
    send_latent = pool_latent[local_slot]
    send_rotary = pool_rope[local_slot]
    fetched_latent, fetched_rotary = (
        lax.all_to_all(send_latent, "pool", split_axis=0, concat_axis=0, tiled=True),
        lax.all_to_all(send_rotary, "pool", split_axis=0, concat_axis=0, tiled=True),
    )
    own_row = lax.dynamic_index_in_dim(source, pool_index, 0, keepdims=False)
    senders = jnp.arange(pool_count, dtype=jnp.int32)
    arrivals = jnp.sum((own_row[None, :] == senders[:, None]).astype(jnp.int32), axis=1)
    live_blocks = block_rank[None, :] < arrivals[:, None]
    rest_len = pool_count * CAP * BLK
    rest_latent = fetched_latent.reshape(rest_len, KV)
    rest_rotary = jnp.transpose(
        fetched_rotary.reshape(pool_count * CAP, ROPE, BLK), (1, 0, 2)
    ).reshape(ROPE, rest_len)
    rest_live = jnp.broadcast_to(live_blocks[:, :, None], (pool_count, CAP, BLK)).reshape(rest_len)
    resident_count = resident_len[0]
    suffix_count = suffix_len[0]
    positions = jnp.arange(SUF, dtype=jnp.int32)
    resident_live = jnp.arange(RES, dtype=jnp.int32) < resident_count
    suffix_live = (positions[None, :] <= positions[:, None]) & (positions[None, :] < suffix_count)
    valid = jnp.concatenate(
        [
            jnp.broadcast_to(rest_live[None, :], (SUF, rest_len)),
            jnp.broadcast_to(resident_live[None, :], (SUF, RES)),
            suffix_live,
        ],
        axis=1,
    )
    key_latent = jnp.concatenate([rest_latent, resident_latent[0], new_latent], axis=0)
    key_rotary = jnp.concatenate([rest_rotary, resident_rope[0], new_rope], axis=1)
    head_local = q_nope.shape[1] // NOPE
    groups = head_local // group_heads
    query_nope = q_nope.reshape(SUF, head_local, NOPE)
    query_abs = jnp.einsum(
        "thn,hnc->thc", query_nope, w_uk, preferred_element_type=jnp.float32
    ).astype(jnp.bfloat16)
    query_rot = q_rope.reshape(SUF, head_local, ROPE)
    grouped_abs = jnp.transpose(query_abs.reshape(SUF, groups, group_heads, KV), (1, 0, 2, 3))
    grouped_rot = jnp.transpose(query_rot.reshape(SUF, groups, group_heads, ROPE), (1, 0, 2, 3))
    score_scale = (NOPE + ROPE) ** (-0.5)
    context = lax.map(
        lambda operands: attend_group(
            operands[0], operands[1], key_latent, key_rotary, valid, score_scale
        ),
        (grouped_abs, grouped_rot),
    )
    head_out = jnp.einsum(
        "gthc,ghcv->tghv",
        context,
        w_uv.reshape(groups, group_heads, KV, VD),
        preferred_element_type=jnp.float32,
    )
    head_out = head_out.reshape(SUF, head_local * VD).astype(jnp.bfloat16)
    partial_out = jnp.dot(head_out, w_out, preferred_element_type=jnp.float32)
    summed = lax.psum_scatter(
        partial_out.astype(jnp.bfloat16), "head", scatter_dimension=1, tiled=True
    ).astype(jnp.float32)
    summed = jnp.where((positions < suffix_count)[:, None], summed, jnp.zeros_like(summed))
    return summed.astype(jnp.bfloat16)


def solution(mesh):
    placed = (
        P("pool", "head"),
        P("pool", "head"),
        P("pool", None),
        P(None, "pool"),
        P("pool", None, None),
        P("pool", None, None),
        P("pool", None, None),
        P("pool", None),
        P(),
        P("pool"),
        P("pool"),
        P("head", None, None),
        P("head", None, None),
        P("head", None),
    )
    return jax.shard_map(
        body, mesh=mesh, in_specs=placed, out_specs=P("pool", "head"), check_vma=False
    )
```

profile of v0, /device:TPU:4, one launch (start us, length us, event | category | flops | bytes accessed | tf_op | source)
XLA Modules:
  0.0 168.7 jit_solution(4122023527110117217)
XLA Ops:
  9.3 1.9 %gather_fusion.1 = bf16[32,4096]{1,0:T(8,128)(2,1)S(1)} fusion(bf16[32,4096]{1,0:T(8,128)(2,1)} %param.23, s32[1024]{0:T(1024)S(1)} %pad_clamp_fusion), kind=kCustom, calls=%fused_computation.1 | custom fusion | bytes 524416 | tf_op jit(solution)/shard_map/gather | solution.py:62
  12.1 7.5 %all-to-all-start.1 = ((bf16[16,2,4096]{2,1,0:T(2,128)(2,1)}), bf16[16,2,4096]{2,1,0:T(2,128)(2,1)S(1)}, u32[]{:S(2)}, u32[]{:S(2)}) async-start(bf16[16,2,4096]{2,1,0:T(2,128)(2,1)} %reshape.89), calls=%async_computation.1 | async-start | bytes 524288 | tf_op jit(solution)/shard_map/all_to_all | solution.py:65
  19.6 2.0 %gather_fusion = bf16[32,64,512]{2,1,0:T(8,128)(2,1)} fusion(bf16[32,64,512]{2,1,0:T(8,128)(2,1)S(1)} %copy-done, s32[1024]{0:T(1024)S(1)} %pad_clamp_fusion), kind=kCustom, calls=%fused_computation | custom fusion | bytes 4194432 | tf_op jit(solution)/shard_map/gather | solution.py:61
  21.7 4.2 %all-to-all-done.1 = bf16[16,2,4096]{2,1,0:T(2,128)(2,1)S(1)} async-done(((bf16[16,2,4096]{2,1,0:T(2,128)(2,1)}), bf16[16,2,4096]{2,1,0:T(2,128)(2,1)S(1)}, u32[]{:S(2)}, u32[]{:S(2)}) %all-to-all-start.1) | async-done | bytes 262176 | tf_op jit(solution)/shard_map/all_to_all | solution.py:65
  26.0 6.5 %all-to-all-start = ((bf16[16,2,64,512]{3,2,1,0:T(8,128)(2,1)}), bf16[16,2,64,512]{3,2,1,0:T(8,128)(2,1)}, u32[]{:S(2)}, u32[]{:S(2)}) async-start(bf16[16,2,64,512]{3,2,1,0:T(8,128)(2,1)} %bitcast.81), calls=%async_computation | async-start | bytes 4194304 | tf_op jit(solution)/shard_map/all_to_all | solution.py:64
  34.0 3.2 %convolution_convert_fusion.1 = bf16[8,512,256]{2,1,0:T(8,128)(2,1)} fusion(bf16[8,128,512]{2,1,0:T(8,128)(2,1)S(1)} %copy-done.3, bf16[256,1024]{1,0:T(8,128)(2,1)} %param.16), kind=kOutput, calls=%fused_computation.24 | convolution fusion | flops 269484032 | bytes 3670016 | tf_op jit(solution)/shard_map/thn,hnc->thc/dot_general | solution.py:95
  37.2 4.2 %copy.31 = bf16[256,2,4,512]{3,0,2,1:T(8,128)(2,1)} copy(bf16[256,2,4,512]{0,3,2,1:T(8,128)(2,1)} %bitcast.80) | data formatting | bytes 4194304 | tf_op jit(solution)/shard_map/reshape | solution.py:99
  43.7 2.2 %copy.44 = bf16[32,64,64]{2,0,1:T(8,128)(2,1)} copy(bf16[32,64,64]{2,1,0:T(8,128)(2,1)} %reshape.77) | data formatting | bytes 524288 | tf_op jit(solution)/shard_map/reshape | solution.py:74
  45.9 1.5 reshape.78
  47.4 11.5 %all-to-all-done = bf16[16,2,64,512]{3,2,1,0:T(8,128)(2,1)} async-done(((bf16[16,2,64,512]{3,2,1,0:T(8,128)(2,1)}), bf16[16,2,64,512]{3,2,1,0:T(8,128)(2,1)}, u32[]{:S(2)}, u32[]{:S(2)}) %all-to-all-start) | async-done | bytes 2097184 | tf_op jit(solution)/shard_map/all_to_all | solution.py:64
  58.9 3.5 %pad_maximum_fusion = bf16[2560,512]{1,0:T(8,128)(2,1)} fusion(bf16[256,512]{1,0:T(8,128)(2,1)} %param.18, bf16[256,512]{1,0:T(8,128)(2,1)} %bitcast.87, bf16[2048,512]{1,0:T(8,128)(2,1)} %bitcast.13), kind=kLoop, calls=%fused_computation.22 | loop fusion | flops 7864320 | bytes 5242880 | tf_op jit(solution)/shard_map/concatenate | solution.py:90
  62.4 27.3 %while.10 = (s32[]{:T(128)}, bf16[2,256,4,512]{3,1,2,0:T(8,128)(2,1)}, pred[256,2560]{1,0:T(8,128)(4,1)S(1)}, bf16[2,256,4,512]{3,1,2,0:T(8,128)(2,1)}, bf16[256...) while((s32[]{:T(128)}, ...), condition=%wide.region_6.7_spmd, body=%wide.region_3.6_spmd.sunk | while | flops 5726271488 | bytes 72438928 | solution.py:102
  62.4 5.0 %fusion.54 = f32[256,4,2560]{2,0,1:T(8,128)S(1)} fusion(bf16[2560,512]{1,0:T(8,128)(2,1)} %get-tuple-element.128, bf16[2,256,4,512]{3,1,2,0:T(8,128)(2,1)} %get-tuple-element.127, s32[]{:T(128)} %get-tuple-element.116), kind=kOutput, calls=%fused_computation.9.clone.1 | convolution fusion | flops 2684354560 | bytes 14156288 | tf_op jit(solution)/shard_map/while/body/eval_jaxpr/tgc,lc->tgl/dot_general | solution.py:20
  67.4 2.9 %fusion.55 = (f32[256,4]{0,1:T(4,128)S(1)}, f32[256,4,2560]{2,0,1:T(8,128)S(1)}) fusion(f32[256,4,2560]{2,0,1:T(8,128)S(1)} %fusion.54, bf16[64,2560]{1,0:T(8,128)(2,1)S(1)} %get-tuple-element.130, bf16[2,256,4,64]{1,3,2,0:T(8,128)(2,1)S(1)} %copy-done.1, s32[]{:T(128)} %get-tuple-element.116, pred[256,2560]{1,0:T(8,128)(4,1)S(1)} %get-tuple-element.126), kind=kOutput, calls=%fused_computation.51.clone.1 | convolution fusion | flops 346029056 | bytes 22089732 | tf_op jit(solution)/shard_map/while/body/eval_jaxpr/tgr,rl->tgl/dot_general | solution.py:21
  70.3 1.6 fusion.56
  72.1 4.0 %fusion.57 = bf16[2,256,4,512]{3,1,2,0:T(8,128)(2,1)} fusion(bf16[2,256,4,512]{3,1,2,0:T(8,128)(2,1)} %get-tuple-element.117, s32[]{:T(128)} %get-tuple-element.116, bf16[2560,512]{1,0:T(8,128)(2,1)S(1)} %copy-done.2, f32[256,4,2560]{2,0,1:T(8,128)S(1)} %get-tuple-element.106, f32[256,4]{0,1:T(4,128)S(1)} %get-tuple-element.107, ...), kind=kOutput, calls=%fused_computation.13.clone.1 | convolution fusion | flops 2690646016 | bytes 14164480 | tf_op jit(solution)/shard_map/while/body/eval_jaxpr/tgl,lc->tgc/dot_general | solution.py:29
  76.0 5.0 %fusion.54 = f32[256,4,2560]{2,0,1:T(8,128)S(1)} fusion(bf16[2560,512]{1,0:T(8,128)(2,1)} %get-tuple-element.128, bf16[2,256,4,512]{3,1,2,0:T(8,128)(2,1)} %get-tuple-element.127, s32[]{:T(128)} %get-tuple-element.116), kind=kOutput, calls=%fused_computation.9.clone.1 | convolution fusion | flops 2684354560 | bytes 14156288 | tf_op jit(solution)/shard_map/while/body/eval_jaxpr/tgc,lc->tgl/dot_general | solution.py:20
  81.1 2.9 %fusion.55 = (f32[256,4]{0,1:T(4,128)S(1)}, f32[256,4,2560]{2,0,1:T(8,128)S(1)}) fusion(f32[256,4,2560]{2,0,1:T(8,128)S(1)} %fusion.54, bf16[64,2560]{1,0:T(8,128)(2,1)S(1)} %get-tuple-element.130, bf16[2,256,4,64]{1,3,2,0:T(8,128)(2,1)S(1)} %copy-done.1, s32[]{:T(128)} %get-tuple-element.116, pred[256,2560]{1,0:T(8,128)(4,1)S(1)} %get-tuple-element.126), kind=kOutput, calls=%fused_computation.51.clone.1 | convolution fusion | flops 346029056 | bytes 22089732 | tf_op jit(solution)/shard_map/while/body/eval_jaxpr/tgr,rl->tgl/dot_general | solution.py:21
  84.0 1.6 fusion.56
  85.7 4.0 %fusion.57 = bf16[2,256,4,512]{3,1,2,0:T(8,128)(2,1)} fusion(bf16[2,256,4,512]{3,1,2,0:T(8,128)(2,1)} %get-tuple-element.117, s32[]{:T(128)} %get-tuple-element.116, bf16[2560,512]{1,0:T(8,128)(2,1)S(1)} %copy-done.2, f32[256,4,2560]{2,0,1:T(8,128)S(1)} %get-tuple-element.106, f32[256,4]{0,1:T(4,128)S(1)} %get-tuple-element.107, ...), kind=kOutput, calls=%fused_computation.13.clone.1 | convolution fusion | flops 2690646016 | bytes 14164480 | tf_op jit(solution)/shard_map/while/body/eval_jaxpr/tgl,lc->tgc/dot_general | solution.py:29
  89.7 2.7 %convolution_convert_fusion.2 = bf16[2,4,256,128]{2,3,1,0:T(8,128)(2,1)S(1)} fusion(bf16[2,256,4,512]{3,1,2,0:T(8,128)(2,1)} %get-tuple-element.42, bf16[2,4,512,128]{3,2,1,0:T(8,128)(2,1)} %bitcast.85), kind=kOutput, calls=%fused_computation.25 | convolution fusion | flops 268697600 | bytes 3670016 | tf_op jit(solution)/shard_map/gthc,ghcv->tghv/dot_general | solution.py:108
  92.4 7.4 %convolution_convert_fusion = bf16[256,3584]{0,1:T(8,128)(2,1)} fusion(bf16[256,1024]{0,1:T(8,128)(2,1)S(1)} %bitcast.86, bf16[1024,3584]{1,0:T(8,128)(2,1)} %param.29), kind=kOutput, calls=%fused_computation.21 | convolution fusion | flops 1879965696 | bytes 9699328 | tf_op jit(solution)/shard_map/dot_general | solution.py:115
  99.8 60.4 %reduce-scatter.2.cloned.1.call-done = bf16[256,224]{0,1:T(8,128)(2,1)} async-done(((bf16[256,3584]{0,1:T(8,128)(2,1)}), bf16[256,224]{0,1:T(8,128)(2,1)}) %reduce-scatter.2.cloned.1.call-update) | async-done | bytes 114704 | tf_op jit(solution)/shard_map/reduce_scatter | solution.py:116
  160.3 1.6 select_convert_fusion
  (44 shorter events, 6.7 us)
Async XLA Ops:
  6.5 13.1 %copy-start = (bf16[32,64,512]{2,1,0:T(8,128)(2,1)S(1)}, bf16[32,64,512]{2,1,0:T(8,128)(2,1)}, u32[]{:S(2)}) copy-start(bf16[32,64,512]{2,1,0:T(8,128)(2,1)} %param.22) | copy-start | bytes 6291460
  12.1 13.8 %all-to-all-start.1 = ((bf16[16,2,4096]{2,1,0:T(2,128)(2,1)}), bf16[16,2,4096]{2,1,0:T(2,128)(2,1)S(1)}, u32[]{:S(2)}, u32[]{:S(2)}) async-start(bf16[16,2,4096]{2,1,0:T(2,128)(2,1)} %reshape.89), calls=%async_computation.1 | async-start | bytes 524288 | tf_op jit(solution)/shard_map/all_to_all | solution.py:65
  21.6 12.4 %copy-start.3 = (bf16[8,128,512]{2,1,0:T(8,128)(2,1)S(1)}, bf16[8,128,512]{2,1,0:T(8,128)(2,1)}, u32[]{:S(2)}) copy-start(bf16[8,128,512]{2,1,0:T(8,128)(2,1)} %param.27) | copy-start | bytes 3145732
  26.0 33.0 %all-to-all-start = ((bf16[16,2,64,512]{3,2,1,0:T(8,128)(2,1)}), bf16[16,2,64,512]{3,2,1,0:T(8,128)(2,1)}, u32[]{:S(2)}, u32[]{:S(2)}) async-start(bf16[16,2,64,512]{3,2,1,0:T(8,128)(2,1)} %bitcast.81), calls=%async_computation | async-start | bytes 4194304 | tf_op jit(solution)/shard_map/all_to_all | solution.py:64
  32.4 127.8 %reduce-scatter.2.cloned.1.call-start = ((), (), s32[]{:S(2)}) async-start(), calls=%async_computation.3 | async-start | bytes 1949696 | tf_op jit(solution)/shard_map/reduce_scatter | solution.py:116
  37.2 4.2 %copy-start.4 = (bf16[256,512]{1,0:T(8,128)(2,1)S(1)}, bf16[256,512]{1,0:T(8,128)(2,1)}, u32[]{:S(2)}) copy-start(bf16[256,512]{1,0:T(8,128)(2,1)} %param.17) | copy-start | bytes 786436
  41.4 6.0 %copy-start.5 = (bf16[64,256]{1,0:T(8,128)(2,1)S(1)}, bf16[64,256]{1,0:T(8,128)(2,1)}, u32[]{:S(2)}) copy-start(bf16[64,256]{1,0:T(8,128)(2,1)} %param.19) | copy-start | bytes 98308
  41.4 6.0 %copy-start.6 = (bf16[1,64,256]{2,1,0:T(8,128)(2,1)S(1)}, bf16[1,64,256]{2,1,0:T(8,128)(2,1)}, u32[]{:S(2)}) copy-start(bf16[1,64,256]{2,1,0:T(8,128)(2,1)} %param.21) | copy-start | bytes 98308
  62.4 5.0 %copy-start.1 = (bf16[2,256,4,64]{1,3,2,0:T(8,128)(2,1)S(1)}, bf16[2,256,4,64]{1,3,2,0:T(8,128)(2,1)}, u32[]{:S(2)}) copy-start(bf16[2,256,4,64]{1,3,2,0:T(8,128)(2,1)} %get-tuple-element.129) | copy-start | bytes 786436 | tf_op jit(solution)/shard_map/while
  70.3 1.7 %copy-start.2 = (bf16[2560,512]{1,0:T(8,128)(2,1)S(1)}, bf16[2560,512]{1,0:T(8,128)(2,1)}, u32[]{:S(2)}) copy-start(bf16[2560,512]{1,0:T(8,128)(2,1)} %get-tuple-element.128) | copy-start | bytes 7864324 | tf_op jit(solution)/shard_map/while
  76.0 5.0 %copy-start.1 = (bf16[2,256,4,64]{1,3,2,0:T(8,128)(2,1)S(1)}, bf16[2,256,4,64]{1,3,2,0:T(8,128)(2,1)}, u32[]{:S(2)}) copy-start(bf16[2,256,4,64]{1,3,2,0:T(8,128)(2,1)} %get-tuple-element.129) | copy-start | bytes 786436 | tf_op jit(solution)/shard_map/while
  84.0 1.7 %copy-start.2 = (bf16[2560,512]{1,0:T(8,128)(2,1)S(1)}, bf16[2560,512]{1,0:T(8,128)(2,1)}, u32[]{:S(2)}) copy-start(bf16[2560,512]{1,0:T(8,128)(2,1)} %get-tuple-element.128) | copy-start | bytes 7864324 | tf_op jit(solution)/shard_map/while
Sparse Core Ops, SparseCore 0:
  99.9 60.2 reduce-scatter.1
where the time goes:
time: 169 us
  waiting for transfers between devices  76.1 us (45%)
  matrix products  37 us (22%)
  local copies, waits for them, and re-layouts  15.5 us (9%)
  between operations  14.8 us (9%)
  starting transfers between devices  13.9 us (8%)
  other arithmetic  11.2 us (7%)
    reduce_scatter x1, waiting for transfers between devices, body(): lax.psum_scatter(partial_out.astype(jnp.bfloat16), 'head', scatter_dimens...  60.4 us
    all_to_all x1, waiting for transfers between devices, body(): lax.all_to_all(send_latent, 'pool', split_axis=0, concat_axis=0, tiled=True)  11.5 us
    dot_general x2, matrix products, attend_group(): jnp.einsum('tgc,lc->tgl', query_abs, key_latent, preferred_element_type=j...  10 us
    dot_general x2, matrix products, attend_group(): jnp.einsum('tgl,lc->tgc', weights, key_latent, preferred_element_type=jnp...  8 us
    all_to_all x1, starting transfers between devices, body(): lax.all_to_all(send_rotary, 'pool', split_axis=0, concat_axis=0, tiled=True)  7.45 us
    dot_general x1, matrix products, body(): partial_out = jnp.dot(head_out, w_out, preferred_element_type=jnp.float32)  7.39 us
    all_to_all x1, starting transfers between devices, body(): lax.all_to_all(send_latent, 'pool', split_axis=0, concat_axis=0, tiled=True)  6.45 us
    dot_general x2, matrix products, attend_group(): jnp.einsum('tgr,rl->tgl', query_rot, key_rotary, preferred_element_type=j...  5.76 us
  transfers between devices with their start and end apart: 3, of which 3 were waited for; matrix products, arithmetic and copies ran while one was open for 9% of the time, Pallas kernels for 0%

commit v1 on v0

v1 whole, which is shorter than its diff:
```python
import functools
import math

import jax
import jax.numpy as jnp
from jax import lax
from jax.experimental import pallas as pl
from jax.experimental.pallas import tpu as pltpu
from jax.sharding import PartitionSpec as P

MESH = pl.DeviceIdType.MESH
NOPE = 128
ROPE = 64
KV = 512
BLK = 64
HL = 8
SUF = 256
RES = 256
SLOTS = 32
NBMAX = 32
REST = NBMAX * BLK
KEYS = REST + RES + SUF
DW = 3584
COLS = 224
NZ = 8
BIG = 1e30
FACTOR = math.log2(math.e) / math.sqrt(NOPE + ROPE)
MSG = BLK * KV // 128 + ROPE * BLK // 128
LAT = BLK * KV // 128
HALF = 128
CHUNKS = SUF // HALF
PR = HALF // 4

f32 = jnp.float32
bf16 = jnp.bfloat16


def dot(a, b):
    return jnp.dot(a, b, preferred_element_type=f32)


def kernel(
    q_nope, q_rope, new_latent, new_rope, res_latent, res_rope, pool_latent, pool_rope,
    table, res_len, suf_len, w_uk, w_uv, w_out,
    out,
    pool_l, pool_r, rope_f, send_buf, kb, loc_l, loc_r, wuk, wuv, wout, qn, qr, qx,
    kn, krm, val, ho, po, share, pair_in, right_in, left_in,
    load_sem, xy_send, z_send, c_send, kb_recv,
    pair_send, pair_recv, right_send, right_recv, left_send, left_recv,
):
    pool = lax.axis_index("pool")
    head = lax.axis_index("head")
    mx, my = pool // 4, pool % 4
    z, core = head // 2, head % 2
    zp = z % 2
    znext = lax.rem(z + 1, NZ) * 2 + core
    zprev = lax.rem(z + NZ - 1, NZ) * 2 + core
    partner = z * 2 + (1 - core)
    zkey = lax.rem(z + 1 + core * (NZ - 2), NZ) * 2 + core

    def offset_peer(o):
        dx = o // 2
        dy = 2 * (o % 2) + (dx + zp) % 2
        return ((mx + dx) % 4) * 4 + (my + dy) % 4

    loads = []

    def load(src, dst):
        copy = pltpu.make_async_copy(src, dst, load_sem.at[len(loads)])
        copy.start()
        loads.append(copy)
        return copy

    ld_pool_r = load(pool_rope, pool_r)
    ld_pool_l = load(pool_latent, pool_l)

    barrier = pltpu.get_barrier_semaphore()
    for o in range(8):
        if o == 0:
            @pl.when(zp == 1)
            def _():
                pl.semaphore_signal(barrier, inc=1, device_id=(offset_peer(0), head), device_id_type=MESH)
        else:
            pl.semaphore_signal(barrier, inc=1, device_id=(offset_peer(o), head), device_id_type=MESH)
    for other in (znext, zprev, partner):
        pl.semaphore_signal(barrier, inc=1, device_id=(pool, other), device_id_type=MESH)

    ld_res_l = load(res_latent.at[0], loc_l.at[pl.ds(0, RES)])
    ld_new_l = load(new_latent, loc_l.at[pl.ds(RES, SUF)])
    ld_uk = load(w_uk, wuk)
    ld_uv = [load(w_uv.at[h], wuv.at[:, pl.ds(h * 128, 128)]) for h in range(HL)]
    ld_res_r = load(res_rope.at[0], loc_r.at[:, pl.ds(0, RES)])
    ld_new_r = load(new_rope, loc_r.at[:, pl.ds(RES, SUF)])
    ld_qr = load(q_rope, qr)
    ld_qn = load(q_nope, qn)
    ld_out = load(w_out, wout)

    low = pool * SLOTS
    slots = []
    for o in range(8):
        row = offset_peer(o)
        found = jnp.int32(0)
        for j in range(NBMAX):
            at = j + (1 - core) * (NBMAX - 1 - 2 * j)
            rel = table[row, at] - low
            found = jnp.where((rel >= 0) & (rel < SLOTS), rel, found)
        slots.append(found)

    pick_row = lax.broadcasted_iota(jnp.int32, (16, SLOTS), 0)
    pick_lane = lax.broadcasted_iota(jnp.int32, (16, SLOTS), 1)
    pick = jnp.zeros((16, SLOTS), f32)
    for o in range(8):
        pick = jnp.where((pick_row == o) & (pick_lane == slots[o]), 1.0, pick)
    ld_pool_r.wait()
    chosen = dot(pick.astype(bf16), pool_r[...])
    for r in range(32):
        rope_f[pl.ds(r, 8, stride=32), :] = chosen[0:8, r * 128 : r * 128 + 128]
    ld_pool_l.wait()
    for o in range(8):
        block = pool_l[slots[o]]
        for j in range(4):
            send_buf[o, j * BLK : (j + 1) * BLK, :] = block[:, j * 128 : j * 128 + 128]
        send_buf[o, LAT:MSG, :] = rope_f[o * 32 : o * 32 + 32, :].astype(bf16)

    pl.semaphore_wait(barrier, 10 + zp)

    def remote(src, dst, send, recv, device):
        return pltpu.make_async_remote_copy(
            src_ref=src, dst_ref=dst, send_sem=send, recv_sem=recv,
            device_id=device, device_id_type=MESH,
        )

    def xy(o):
        return remote(send_buf.at[o], kb.at[0, 0, o], xy_send.at[o], kb_recv.at[0, 0, o], (offset_peer(o), head))

    def over_z(o):
        return remote(kb.at[0, 0, o], kb.at[1, 0, o], z_send.at[o], kb_recv.at[1, 0, o], (pool, zkey))

    def over_core(rz, o):
        return remote(kb.at[rz, 0, o], kb.at[rz, 1, o], c_send.at[rz, o], kb_recv.at[rz, 1, o], (pool, partner))

    @pl.when(zp == 1)
    def _():
        xy(0).start()

    for o in range(1, 8):
        xy(o).start()

    @pl.when(zp == 0)
    def _():
        kb[0, 0, 0] = send_buf[0]

    def arrive_xy(o):
        if o == 0:
            @pl.when(zp == 1)
            def _():
                xy(0).wait_recv()
        else:
            xy(o).wait_recv()
        over_z(o).start()
        over_core(0, o).start()

    def arrive_z(o):
        over_z(o).wait_recv()
        over_core(1, o).start()

    def arrive_core(rz, o):
        over_core(rz, o).wait_recv()

    group = lax.broadcasted_iota(jnp.int32, (16, 128), 0)
    lane = lax.broadcasted_iota(jnp.int32, (16, 128), 1)
    blk = 2 * group + lane // BLK
    b_z, b_c, b_o = blk // 16, (blk // 8) % 2, blk % 8
    b_dx = b_o // 2
    b_dy = 2 * (b_o % 2) + (b_dx + zp + b_z) % 2
    b_src = ((mx - b_dx + 4) % 4) * 4 + (my - b_dy + 4) % 4
    b_rank = (core + b_c) % 2
    b_low = b_src * SLOTS
    count = jnp.zeros((16, 128), jnp.int32)
    for j in range(NBMAX):
        listed = table[pool, j]
        count = count + jnp.where((listed >= b_low) & (listed < b_low + SLOTS), 1, 0)
    rest_bias = jnp.where(count > b_rank, 0.0, -BIG)
    first_row = lax.broadcasted_iota(jnp.int32, (64, 128), 0) == 0

    def put_bias(g, row):
        krm[64:128, g * 128 : (g + 1) * 128] = jnp.where(first_row, row, 0.0).astype(bf16)

    for g in range(16):
        put_bias(g, rest_bias[g : g + 1, :])
    lane1 = lax.broadcasted_iota(jnp.int32, (1, 128), 1)
    for g in range(4):
        limit = res_len[0] if g < 2 else suf_len[0]
        put_bias(16 + g, jnp.where(lane1 + (g % 2) * 128 < limit, 0.0, -BIG))

    def expand(lat, at, n):
        kn[:, at : at + n] = (
            lax.dot_general(
                wuk[...].reshape(HL * NOPE, KV), lat, (((1,), (1,)), ((), ())), preferred_element_type=f32
            )
            * FACTOR
        ).astype(bf16)
        val[at : at + n, :] = dot(lat, wuv[...]).astype(bf16)

    def expand_rest(rz, rc, o):
        lat = jnp.concatenate(
            [kb[rz, rc, o : o + 4, j * BLK : (j + 1) * BLK, :].reshape(4 * BLK, 128) for j in range(4)], axis=1
        )
        at = ((rz * 2 + rc) * 8 + o) * BLK
        expand(lat, at, 4 * BLK)
        for i in range(0, 4, 2):
            a = kb[rz, rc, o + i, LAT:MSG, :].astype(f32) * FACTOR
            b = kb[rz, rc, o + i + 1, LAT:MSG, :].astype(f32) * FACTOR
            even = jnp.concatenate([a[:, :BLK], b[:, :BLK]], axis=1)
            odd = jnp.concatenate([a[:, BLK:], b[:, BLK:]], axis=1)
            krm[0:64, at + i * BLK : at + (i + 2) * BLK] = jnp.concatenate([even, odd], axis=0).astype(bf16)

    ld_res_l.wait()
    ld_uk.wait()
    for copy in ld_uv:
        copy.wait()
    expand(loc_l[0:RES, :], REST, RES)
    for o in range(0, 4):
        arrive_xy(o)
    ld_new_l.wait()
    expand(loc_l[RES : RES + SUF, :], REST + RES, SUF)
    for o in range(4, 8):
        arrive_xy(o)

    ld_res_r.wait()
    ld_new_r.wait()
    perm_r = lax.broadcasted_iota(jnp.int32, (64, 64), 0)
    perm_c = lax.broadcasted_iota(jnp.int32, (64, 64), 1)
    perm = jnp.where(perm_c == 2 * (perm_r % 32) + perm_r // 32, 1.0, 0.0).astype(bf16)
    krm[0:64, REST:KEYS] = (dot(perm, loc_r[...]) * FACTOR).astype(bf16)

    expand_rest(0, 0, 0)
    for o in range(0, 4):
        arrive_z(o)
    expand_rest(0, 0, 4)
    for o in range(0, 4):
        arrive_core(0, o)
    expand_rest(0, 1, 0)
    for o in range(4, 8):
        arrive_z(o)
    for o in range(4, 8):
        arrive_core(0, o)
    expand_rest(0, 1, 4)

    ld_qr.wait()
    ld_qn.wait()
    lane_r = lax.broadcasted_iota(jnp.int32, (128, 128), 0)
    lane_c = lax.broadcasted_iota(jnp.int32, (128, 128), 1)
    one_lane = lax.broadcasted_iota(jnp.int32, (SUF, 128), 1) == 64
    for h in range(HL):
        spread = jnp.where(
            (lane_c < 64) & (lane_r == (h % 2) * 64 + 2 * (lane_c % 32) + lane_c // 32), 1.0, 0.0
        ).astype(bf16)
        turned = dot(qr[:, (h // 2) * 128 : (h // 2) * 128 + 128], spread)
        qx[h] = jnp.where(one_lane, 1.0, turned).astype(bf16)

    expand_rest(1, 0, 0)
    expand_rest(1, 0, 4)
    for o in range(0, 4):
        arrive_core(1, o)
    expand_rest(1, 1, 0)
    for o in range(4, 8):
        arrive_core(1, o)
    expand_rest(1, 1, 4)

    def pair(c):
        return remote(
            share.at[c, 1], pair_in.at[c], pair_send.at[c], pair_recv.at[c], (pool, partner)
        )

    def right(c, s):
        return remote(
            share.at[c, 0, lax.rem(z + 4 - s, NZ)], right_in.at[c, s], right_send.at[c, s],
            right_recv.at[c, s], (pool, znext),
        )

    def left(c, s):
        return remote(
            share.at[c, 0, lax.rem(z + 5 + s, NZ)], left_in.at[c, s], left_send.at[c, s],
            left_recv.at[c, s], (pool, zprev),
        )

    def ring(c, s):
        if s == 0:
            pair(c).wait_recv()
            for k in range(NZ):
                share[c, 0, k] = (share[c, 0, k].astype(f32) + pair_in[c, k].astype(f32)).astype(bf16)
        else:
            right(c, s - 1).wait_recv()
            k = lax.rem(z + 4 - s, NZ)
            share[c, 0, k] = (share[c, 0, k].astype(f32) + right_in[c, s - 1].astype(f32)).astype(bf16)
            if s < 3:
                left(c, s - 1).wait_recv()
                k = lax.rem(z + 5 + s, NZ)
                share[c, 0, k] = (share[c, 0, k].astype(f32) + left_in[c, s - 1].astype(f32)).astype(bf16)
        right(c, s).start()
        if s < 3:
            left(c, s).start()

    def finish(c):
        right(c, 3).wait_recv()
        left(c, 2).wait_recv()
        total = share[c, 0, z].astype(f32) + right_in[c, 3].astype(f32) + left_in[c, 2].astype(f32)
        for g in range(4):
            rows = lax.broadcasted_iota(jnp.int32, (PR, COLS), 0) + (c * HALF + g * PR)
            part = jnp.where(rows < suf_len[0], total[:, g * COLS : (g + 1) * COLS], 0.0)
            out[c * HALF + g * PR : c * HALF + (g + 1) * PR, :] = part.astype(bf16)

    t_row = lax.broadcasted_iota(jnp.int32, (HALF, SUF), 0)
    u_col = lax.broadcasted_iota(jnp.int32, (HALF, SUF), 1)

    def scores(c, h):
        rows = slice(c * HALF, (c + 1) * HALF)
        q = jnp.concatenate([qn[rows, h * NOPE : (h + 1) * NOPE], qx[h, rows, :]], axis=1)
        k = jnp.concatenate([kn[h * NOPE : (h + 1) * NOPE, :], krm[...]], axis=0)
        s = dot(q, k)
        own = jnp.where(u_col <= t_row + c * HALF, s[:, KEYS - SUF :], -BIG)
        return jnp.concatenate([s[:, : KEYS - SUF], own], axis=1)

    def attend(c, h, s):
        m = jnp.max(s, axis=1, keepdims=True)
        p = jnp.exp2(s - m)
        total = jnp.sum(p, axis=1, keepdims=True)
        o = dot(p.astype(bf16), val[:, h * 128 : (h + 1) * 128])
        ho[c * HALF : (c + 1) * HALF, h * 128 : (h + 1) * 128] = (o * (1.0 / total)).astype(bf16)

    for c in range(CHUNKS):
        s = scores(c, 0)
        for h in range(HL):
            later = scores(c, h + 1) if h + 1 < HL else None
            attend(c, h, s)
            s = later
            if c > 0 and h % 2 == 1:
                ring(c - 1, h // 2)
        if c == 0:
            ld_out.wait()
        for n in range(0, DW, 512):
            po[:, n : n + 512] = dot(ho[c * HALF : (c + 1) * HALF, :], wout[:, n : n + 512]).astype(bf16)
        for k in range(NZ):
            for cc in range(2):
                at = (2 * k + cc) * COLS
                share[c, (core + cc) % 2, k] = jnp.concatenate(
                    [po[g * PR : (g + 1) * PR, at : at + COLS] for g in range(4)], axis=1
                )
        pair(c).start()
        if c > 0:
            finish(c - 1)
    for s in range(4):
        ring(CHUNKS - 1, s)
    finish(CHUNKS - 1)

    @pl.when(zp == 1)
    def _():
        xy(0).wait_send()

    for o in range(8):
        if o > 0:
            xy(o).wait_send()
        over_z(o).wait_send()
        over_core(0, o).wait_send()
        over_core(1, o).wait_send()
    for c in range(CHUNKS):
        pair(c).wait_send()
        for s in range(4):
            right(c, s).wait_send()
            if s < 3:
                left(c, s).wait_send()


def body(*args):
    dma = pltpu.SemaphoreType.DMA
    vmem = lambda *shape, dtype=bf16: pltpu.VMEM(shape, dtype)
    anywhere = pl.BlockSpec(memory_space=pl.ANY)
    smem = pl.BlockSpec(memory_space=pltpu.SMEM)
    return pl.pallas_call(
        kernel,
        out_shape=jax.ShapeDtypeStruct((SUF, COLS), bf16),
        in_specs=[anywhere] * 8 + [smem] * 3 + [anywhere] * 3,
        out_specs=pl.BlockSpec(memory_space=pltpu.VMEM),
        scratch_shapes=[
            vmem(SLOTS, BLK, KV),
            vmem(SLOTS, ROPE * BLK),
            vmem(256, 128, dtype=f32),
            vmem(8, MSG, 128),
            vmem(2, 2, 8, MSG, 128),
            vmem(RES + SUF, KV),
            vmem(ROPE, RES + SUF),
            vmem(HL, NOPE, KV),
            vmem(KV, HL * 128),
            vmem(HL * 128, DW),
            vmem(SUF, HL * NOPE),
            vmem(SUF, HL * ROPE),
            vmem(HL, SUF, 128),
            vmem(HL * NOPE, KEYS),
            vmem(128, KEYS),
            vmem(KEYS, HL * 128),
            vmem(SUF, HL * 128),
            vmem(HALF, DW),
            vmem(CHUNKS, 2, NZ, PR, 4 * COLS),
            vmem(CHUNKS, NZ, PR, 4 * COLS),
            vmem(CHUNKS, 4, PR, 4 * COLS),
            vmem(CHUNKS, 3, PR, 4 * COLS),
            dma((20,)), dma((8,)), dma((8,)), dma((2, 8)), dma((2, 2, 8)),
            dma((CHUNKS,)), dma((CHUNKS,)), dma((CHUNKS, 4)), dma((CHUNKS, 4)), dma((CHUNKS, 3)), dma((CHUNKS, 3)),
        ],
        compiler_params=pltpu.CompilerParams(
            collective_id=0, has_side_effects=True, vmem_limit_bytes=60 * 2**20
        ),
        cost_estimate=pl.CostEstimate(flops=12 * 10**9, bytes_accessed=14 * 10**6, transcendentals=5 * 10**6),
    )(*args)


def solution(mesh):
    placed = (
        P("pool", "head"), P("pool", "head"), P("pool", None), P(None, "pool"),
        P("pool", None, None), P("pool", None, None), P("pool", None, None), P("pool", None),
        P(), P("pool"), P("pool"),
        P("head", None, None), P("head", None, None), P("head", None),
    )
    return jax.shard_map(
        body, mesh=mesh, in_specs=placed, out_specs=P("pool", "head"), check_vma=False
    )
```

time: 169 us -> 70 us (0.41)
  the two profiles are of different devices: /device:TPU:4 before, /device:TPU:2 now
where the time goes in v1:
time: 70 us; the launch traced here: 69.8 us
  Pallas kernels  66.9 us (96%)
  local copies, waits for them, and re-layouts  1.65 us (2%)
  between operations  1.31 us (2%)
    pallas_call x1, Pallas kernels, body(): pl.pallas_call(kernel, out_shape=jax.ShapeDtypeStruct((SUF, COLS), bf16),...  66.9 us
    pallas_call x1, local copies, waits for them, and re-layouts, body(): pl.pallas_call(kernel, out_shape=jax.ShapeDtypeStruct((SUF, COLS), bf16),...  1.65 us

profile of v1, /device:TPU:2, one launch (start us, length us, event | category | flops | bytes accessed | tf_op | source)
XLA Modules:
  0.0 69.8 jit_solution(1324511304409388973)
XLA Ops:
  1.3 66.9 %shard_map.136 = bf16[256,224]{1,0:T(8,128)(2,1)} custom-call(bf16[256,1024]{1,0:T(8,128)(2,1)} %q_nope.1, bf16[256,512]{1,0:T(8,128)(2,1)} %q_rope.1, bf16[256,512]{1,0:T(8,128)(2,1)} %new_latent.1, bf16[64,256]{1,0:T(8,128)(2,1)} %new_rope.1, bf16[1,256,512]{2,1,0:T(8,128)(2,1)} %res_latent.1, bf16[1,64,256]{2,1,0:T(8,128)(2,1)} %res_rope.1, ...), custom_call_target="tpu_custom_call" | custom-call | flops 12000000000 | bytes 14000000 | tf_op jit(solution)/shard_map/pallas_call | solution.py:380
  68.2 1.7 %copy.15 = bf16[256,224]{0,1:T(8,128)(2,1)} copy(bf16[256,224]{1,0:T(8,128)(2,1)} %shard_map.136) | data formatting | bytes 229376 | tf_op jit(solution)/shard_map/pallas_call | solution.py:380

commit v2 on v1

v2 whole, which is shorter than its diff:
```python
import functools
import math

import jax
import jax.numpy as jnp
from jax import lax
from jax.experimental import pallas as pl
from jax.experimental.pallas import tpu as pltpu
from jax.sharding import PartitionSpec as P

MESH = pl.DeviceIdType.MESH
NOPE = 128
ROPE = 64
KV = 512
BLK = 64
HL = 8
SUF = 256
RES = 256
SLOTS = 32
NBMAX = 32
REST = NBMAX * BLK
KEYS = REST + RES + SUF
DW = 3584
COLS = 224
NZ = 8
BIG = 1e30
FACTOR = math.log2(math.e) / math.sqrt(NOPE + ROPE)
MSG = BLK * KV // 128 + ROPE * BLK // 128
LAT = BLK * KV // 128
HALF = 128
CHUNKS = SUF // HALF
PR = HALF // 4
MINE = ((1, 2), (2, 3), (3, 3))
BOTH = ((2, 2), (2, 0), (0, 2), (1, 3), (3, 1), (1, 0), (3, 0), (0, 1), (0, 3))
OFFSETS = MINE + ((0, 0),) + BOTH
SENT = len(OFFSETS)
OWN = 3
EARLY = 2
SPLIT = (8 - EARLY) * 4 * BLK

f32 = jnp.float32
bf16 = jnp.bfloat16


def dot(a, b):
    return jnp.dot(a, b, preferred_element_type=f32)


def kernel(
    q_nope, q_rope, new_latent, new_rope, res_latent, res_rope, pool_latent, pool_rope,
    table, res_len, suf_len, w_uk, w_uv, w_out,
    out,
    pool_l, pool_r, rope_f, send_buf, kb, loc_l, loc_r, wuk, wuv, wout, qn, qr, qx,
    kn, krm, val, o_early, m_early, l_early, ho, po, share, pair_in, sums_in,
    load_sem, xy_send, z_send, c_send, kb_recv,
    pair_send, pair_recv, sums_send, sums_recv,
):
    pool = lax.axis_index("pool")
    head = lax.axis_index("head")
    mx, my = pool // 4, pool % 4
    z, core = head // 2, head % 2
    zp = z % 2
    partner = z * 2 + (1 - core)

    def along_z(n):
        return lax.rem(z + NZ + n, NZ) * 2 + core

    zkey = lax.rem(z + 1 + core * (NZ - 2), NZ) * 2 + core

    def peer(o, way):
        dx, dy = OFFSETS[o]
        if o < OWN:
            way = way * (1 - 2 * zp)
        return ((mx + way * dx + 4) % 4) * 4 + (my + way * dy + 4) % 4

    loads = []

    def load(src, dst):
        copy = pltpu.make_async_copy(src, dst, load_sem.at[len(loads)])
        copy.start()
        loads.append(copy)
        return copy

    ld_pool_r = load(pool_rope, pool_r)
    ld_pool_l = load(pool_latent, pool_l)

    barrier = pltpu.get_barrier_semaphore()
    for o in range(SENT):
        if o != OWN:
            pl.semaphore_signal(barrier, inc=1, device_id=(peer(o, -1), head), device_id_type=MESH)
    for other in (partner, along_z(1), along_z(-1), along_z(2), along_z(-2)):
        pl.semaphore_signal(barrier, inc=1, device_id=(pool, other), device_id_type=MESH)

    ld_res_l = load(res_latent.at[0], loc_l.at[pl.ds(0, RES)])
    ld_new_l = load(new_latent, loc_l.at[pl.ds(RES, SUF)])
    ld_uk = load(w_uk, wuk)
    ld_uv = [load(w_uv.at[h], wuv.at[:, pl.ds(h * 128, 128)]) for h in range(HL)]
    ld_res_r = load(res_rope.at[0], loc_r.at[:, pl.ds(0, RES)])
    ld_new_r = load(new_rope, loc_r.at[:, pl.ds(RES, SUF)])
    ld_qr = load(q_rope, qr)
    ld_qn = load(q_nope, qn)
    ld_out = load(w_out, wout)

    low = pool * SLOTS
    slots = []
    for o in range(SENT):
        row = peer(o, 1)
        found = jnp.int32(0)
        for j in range(NBMAX):
            at = j + (1 - core) * (NBMAX - 1 - 2 * j)
            rel = table[row, at] - low
            found = jnp.where((rel >= 0) & (rel < SLOTS), rel, found)
        slots.append(found)

    pick_row = lax.broadcasted_iota(jnp.int32, (16, SLOTS), 0)
    pick_lane = lax.broadcasted_iota(jnp.int32, (16, SLOTS), 1)
    pick = jnp.zeros((16, SLOTS), f32)
    for o in range(SENT):
        pick = jnp.where((pick_row == o) & (pick_lane == slots[o]), 1.0, pick)
    ld_pool_r.wait()
    chosen = dot(pick.astype(bf16), pool_r[...])
    for r in range(32):
        rope_f[pl.ds(r, 16, stride=32), :] = chosen[:, r * 128 : r * 128 + 128]
    ld_pool_l.wait()
    for o in range(SENT):
        block = pool_l[slots[o]]
        for j in range(4):
            send_buf[o, j * BLK : (j + 1) * BLK, :] = block[:, j * 128 : j * 128 + 128]
        send_buf[o, LAT:MSG, :] = rope_f[o * 32 : o * 32 + 32, :].astype(bf16)
    kb[0, OWN] = send_buf[OWN]

    pl.semaphore_wait(barrier, SENT - 1 + 5)

    def remote(src, dst, send, recv, device):
        return pltpu.make_async_remote_copy(
            src_ref=src, dst_ref=dst, send_sem=send, recv_sem=recv,
            device_id=device, device_id_type=MESH,
        )

    def xy(o):
        return remote(send_buf.at[o], kb.at[0, o], xy_send.at[o], kb_recv.at[0, o], (peer(o, 1), head))

    def over_z(o):
        return remote(kb.at[0, o], kb.at[0, SENT + o], z_send.at[o], kb_recv.at[0, SENT + o], (pool, zkey))

    def over_core(o):
        return remote(kb.at[0, o], kb.at[1, o], c_send.at[o], kb_recv.at[1, o], (pool, partner))

    def arrive(*which):
        for o in which:
            if o >= SENT:
                over_z(o - SENT).wait_recv()
            elif o != OWN:
                xy(o).wait_recv()
            if o < OWN:
                over_z(o).start()
            over_core(o).start()

    def arrive_core(*which):
        for o in which:
            over_core(o).wait_recv()

    def send(*which):
        for o in which:
            xy(o).start()

    def left(*which):
        for o in which:
            xy(o).wait_send()

    send(0, 1, 2, 4, 5, 6)
    over_core(OWN).start()

    group = lax.broadcasted_iota(jnp.int32, (16, 128), 0)
    lane = lax.broadcasted_iota(jnp.int32, (16, 128), 1)
    blk = 2 * group + lane // BLK
    turn = 7 - blk // 4
    b_c, b_o = turn % 2, (turn // 2) * 4 + blk % 4
    b_dx, b_dy = jnp.zeros_like(blk), jnp.zeros_like(blk)
    for o in range(16):
        dx, dy = OFFSETS[o] if o < SENT else OFFSETS[o - SENT]
        way = (1 - 2 * zp) if o < OWN else (2 * zp - 1) if o >= SENT else 1
        b_dx = jnp.where(b_o == o, dx * way, b_dx)
        b_dy = jnp.where(b_o == o, dy * way, b_dy)
    b_src = ((mx - b_dx + 4) % 4) * 4 + (my - b_dy + 4) % 4
    b_rank = (core + b_c) % 2
    b_low = b_src * SLOTS
    count = jnp.zeros((16, 128), jnp.int32)
    for j in range(NBMAX):
        listed = table[pool, j]
        count = count + jnp.where((listed >= b_low) & (listed < b_low + SLOTS), 1, 0)
    rest_bias = jnp.where(count > b_rank, 0.0, -BIG)
    first_row = lax.broadcasted_iota(jnp.int32, (64, 128), 0) == 0

    def put_bias(g, row):
        krm[64:128, g * 128 : (g + 1) * 128] = jnp.where(first_row, row, 0.0).astype(bf16)

    for g in range(16):
        put_bias(g, rest_bias[g : g + 1, :])
    lane1 = lax.broadcasted_iota(jnp.int32, (1, 128), 1)
    for g in range(4):
        limit = res_len[0] if g < 2 else suf_len[0]
        put_bias(16 + g, jnp.where(lane1 + (g % 2) * 128 < limit, 0.0, -BIG))

    def expand(lat, at, n):
        kn[:, at : at + n] = (
            lax.dot_general(
                wuk[...].reshape(HL * NOPE, KV), lat, (((1,), (1,)), ((), ())), preferred_element_type=f32
            )
            * FACTOR
        ).astype(bf16)
        val[at : at + n, :] = dot(lat, wuv[...]).astype(bf16)

    def expand_rest(rc, o):
        lat = jnp.concatenate(
            [kb[rc, o : o + 4, j * BLK : (j + 1) * BLK, :].reshape(4 * BLK, 128) for j in range(4)], axis=1
        )
        at = (7 - (o // 4 * 2 + rc)) * 4 * BLK
        expand(lat, at, 4 * BLK)
        for i in range(0, 4, 2):
            a = kb[rc, o + i, LAT:MSG, :].astype(f32) * FACTOR
            b = kb[rc, o + i + 1, LAT:MSG, :].astype(f32) * FACTOR
            even = jnp.concatenate([a[:, :BLK], b[:, :BLK]], axis=1)
            odd = jnp.concatenate([a[:, BLK:], b[:, BLK:]], axis=1)
            krm[0:64, at + i * BLK : at + (i + 2) * BLK] = jnp.concatenate([even, odd], axis=0).astype(bf16)

    t_row = lax.broadcasted_iota(jnp.int32, (SUF, SUF), 0)
    u_col = lax.broadcasted_iota(jnp.int32, (SUF, SUF), 1)

    def scores(rows, h, keys):
        q = jnp.concatenate([qn[rows, h * NOPE : (h + 1) * NOPE], qx[h, rows, :]], axis=1)
        k = jnp.concatenate([kn[h * NOPE : (h + 1) * NOPE, keys], krm[:, keys]], axis=0)
        return dot(q, k)

    early = slice(SPLIT, KEYS)
    late = slice(0, SPLIT)

    def early_scores(h):
        s = scores(slice(0, SUF), h, early)
        n = KEYS - SUF - SPLIT
        return jnp.concatenate([s[:, :n], jnp.where(u_col <= t_row, s[:, n:], -BIG)], axis=1)

    def attend_early(h, s):
        m = jnp.max(s, axis=1, keepdims=True)
        p = jnp.exp2(s - m)
        total = jnp.sum(p, axis=1, keepdims=True)
        o_early[h] = dot(p.astype(bf16), val[early, h * 128 : (h + 1) * 128])
        m_early[h] = jnp.broadcast_to(m, (SUF, 128))
        l_early[h] = jnp.broadcast_to(total, (SUF, 128))

    def attend(c, h, s):
        rows = slice(c * HALF, (c + 1) * HALF)
        m0 = m_early[h, rows, :]
        m = jnp.maximum(m0, jnp.max(s, axis=1, keepdims=True))
        old = jnp.exp2(m0 - m)
        p = jnp.exp2(s - m[:, 0:1])
        total = l_early[h, rows, :] * old + jnp.sum(p, axis=1, keepdims=True)
        o = o_early[h, rows, :] * old + dot(p.astype(bf16), val[late, h * 128 : (h + 1) * 128])
        ho[rows, h * 128 : (h + 1) * 128] = (o / total).astype(bf16)

    def early_heads(first, last):
        s = early_scores(first)
        for h in range(first, last):
            later = early_scores(h + 1) if h + 1 < last else None
            attend_early(h, s)
            s = later

    ld_res_l.wait()
    ld_uk.wait()
    for copy in ld_uv:
        copy.wait()
    expand(loc_l[0:RES, :], REST, RES)
    left(0, 1, 2)
    send(7, 8, 9)
    ld_new_l.wait()
    expand(loc_l[RES : RES + SUF, :], REST + RES, SUF)
    arrive(0, 1, 2)
    left(4, 5, 6)
    send(10, 11, 12)

    ld_res_r.wait()
    ld_new_r.wait()
    perm_r = lax.broadcasted_iota(jnp.int32, (64, 64), 0)
    perm_c = lax.broadcasted_iota(jnp.int32, (64, 64), 1)
    perm = jnp.where(perm_c == 2 * (perm_r % 32) + perm_r // 32, 1.0, 0.0).astype(bf16)
    krm[0:64, REST:KEYS] = (dot(perm, loc_r[...]) * FACTOR).astype(bf16)

    ld_qr.wait()
    ld_qn.wait()
    lane_r = lax.broadcasted_iota(jnp.int32, (128, 128), 0)
    lane_c = lax.broadcasted_iota(jnp.int32, (128, 128), 1)
    one_lane = lax.broadcasted_iota(jnp.int32, (SUF, 128), 1) == 64
    for h in range(HL):
        spread = jnp.where(
            (lane_c < 64) & (lane_r == (h % 2) * 64 + 2 * (lane_c % 32) + lane_c // 32), 1.0, 0.0
        ).astype(bf16)
        turned = dot(qr[:, (h // 2) * 128 : (h // 2) * 128 + 128], spread)
        qx[h] = jnp.where(one_lane, 1.0, turned).astype(bf16)

    expand_rest(0, 0)
    arrive(4, 5, 6, 7)
    arrive_core(0, 1, 2, OWN)
    expand_rest(1, 0)
    early_heads(0, 3)
    arrive(8, 9, 10, 11)
    expand_rest(0, 4)
    early_heads(3, 6)
    arrive(12, 13, 14, 15)
    arrive_core(4, 5, 6, 7)
    expand_rest(1, 4)
    early_heads(6, 8)
    expand_rest(0, 8)
    arrive_core(8, 9, 10, 11)
    expand_rest(1, 8)
    expand_rest(0, 12)
    arrive_core(12, 13, 14, 15)
    expand_rest(1, 12)

    def pair(c):
        return remote(
            share.at[c, 1], pair_in.at[c], pair_send.at[c], pair_recv.at[c], (pool, partner)
        )

    def hop(c, i):
        way = 1 - 2 * (c % 2)
        of, to = ((4, 2 * way), (3, 1), (-3, -1), (1, 1), (-1, -1), (2, 2), (-2, -2))[i]
        return remote(
            share.at[c, 0, lax.rem(z + NZ + of, NZ)], sums_in.at[c, i], sums_send.at[c, i],
            sums_recv.at[c, i], (pool, along_z(to)),
        )

    def add(c, of, *parts):
        k = lax.rem(z + NZ + of, NZ)
        total = share[c, 0, k].astype(f32)
        for part in parts:
            total = total + part.astype(f32)
        share[c, 0, k] = total.astype(bf16)

    def paired(c, *which):
        for of in which:
            add(c, of, pair_in[c, lax.rem(z + NZ + of, NZ)])

    def step1(c):
        pair(c).wait_recv()
        paired(c, 4, 3, -3)
        for i in range(3):
            hop(c, i).start()
        paired(c, 1, -1)
        for i in range(3, 5):
            hop(c, i).start()
        paired(c, 2, -2, 0)

    def step2(c):
        for i in range(3):
            hop(c, i).wait_recv()
        if c % 2 == 0:
            add(c, 2, sums_in[c, 0], sums_in[c, 1])
            add(c, -2, sums_in[c, 2])
        else:
            add(c, 2, sums_in[c, 1])
            add(c, -2, sums_in[c, 0], sums_in[c, 2])
        for i in range(5, 7):
            hop(c, i).start()

    def finish(c):
        for i in range(3, 7):
            hop(c, i).wait_recv()
        total = share[c, 0, z].astype(f32)
        for i in range(3, 7):
            total = total + sums_in[c, i].astype(f32)
        for g in range(4):
            rows = lax.broadcasted_iota(jnp.int32, (PR, COLS), 0) + (c * HALF + g * PR)
            part = jnp.where(rows < suf_len[0], total[:, g * COLS : (g + 1) * COLS], 0.0)
            out[c * HALF + g * PR : c * HALF + (g + 1) * PR, :] = part.astype(bf16)

    for c in range(CHUNKS):
        rows = slice(c * HALF, (c + 1) * HALF)
        s = scores(rows, 0, late)
        for h in range(HL):
            later = scores(rows, h + 1, late) if h + 1 < HL else None
            attend(c, h, s)
            s = later
            if c > 0 and h == 4:
                step1(c - 1)
        if c == 0:
            ld_out.wait()
        for n in range(0, DW, 512):
            po[:, n : n + 512] = dot(ho[c * HALF : (c + 1) * HALF, :], wout[:, n : n + 512]).astype(bf16)
        for k in range(NZ):
            for cc in range(2):
                at = (2 * k + cc) * COLS
                share[c, (core + cc) % 2, k] = jnp.concatenate(
                    [po[g * PR : (g + 1) * PR, at : at + COLS] for g in range(4)], axis=1
                )
        pair(c).start()
    step1(1)
    step2(0)
    step2(1)
    finish(0)
    finish(1)

    left(7, 8, 9, 10, 11, 12)
    for o in range(OWN):
        over_z(o).wait_send()
    for o in range(16):
        over_core(o).wait_send()
    for c in range(CHUNKS):
        pair(c).wait_send()
        for i in range(7):
            hop(c, i).wait_send()


def body(*args):
    dma = pltpu.SemaphoreType.DMA
    vmem = lambda *shape, dtype=bf16: pltpu.VMEM(shape, dtype)
    anywhere = pl.BlockSpec(memory_space=pl.ANY)
    smem = pl.BlockSpec(memory_space=pltpu.SMEM)
    return pl.pallas_call(
        kernel,
        out_shape=jax.ShapeDtypeStruct((SUF, COLS), bf16),
        in_specs=[anywhere] * 8 + [smem] * 3 + [anywhere] * 3,
        out_specs=pl.BlockSpec(memory_space=pltpu.VMEM),
        scratch_shapes=[
            vmem(SLOTS, BLK, KV),
            vmem(SLOTS, ROPE * BLK),
            vmem(16 * 32, 128, dtype=f32),
            vmem(SENT, MSG, 128),
            vmem(2, 16, MSG, 128),
            vmem(RES + SUF, KV),
            vmem(ROPE, RES + SUF),
            vmem(HL, NOPE, KV),
            vmem(KV, HL * 128),
            vmem(HL * 128, DW),
            vmem(SUF, HL * NOPE),
            vmem(SUF, HL * ROPE),
            vmem(HL, SUF, 128),
            vmem(HL * NOPE, KEYS),
            vmem(128, KEYS),
            vmem(KEYS, HL * 128),
            vmem(HL, SUF, 128, dtype=f32),
            vmem(HL, SUF, 128, dtype=f32),
            vmem(HL, SUF, 128, dtype=f32),
            vmem(SUF, HL * 128),
            vmem(HALF, DW),
            vmem(CHUNKS, 2, NZ, PR, 4 * COLS),
            vmem(CHUNKS, NZ, PR, 4 * COLS),
            vmem(CHUNKS, 7, PR, 4 * COLS),
            dma((20,)), dma((SENT,)), dma((OWN,)), dma((16,)), dma((2, 16)),
            dma((CHUNKS,)), dma((CHUNKS,)), dma((CHUNKS, 7)), dma((CHUNKS, 7)),
        ],
        compiler_params=pltpu.CompilerParams(
            collective_id=0, has_side_effects=True, vmem_limit_bytes=60 * 2**20
        ),
        cost_estimate=pl.CostEstimate(flops=12 * 10**9, bytes_accessed=14 * 10**6, transcendentals=5 * 10**6),
    )(*args)


def solution(mesh):
    placed = (
        P("pool", "head"), P("pool", "head"), P("pool", None), P(None, "pool"),
        P("pool", None, None), P("pool", None, None), P("pool", None, None), P("pool", None),
        P(), P("pool"), P("pool"),
        P("head", None, None), P("head", None, None), P("head", None),
    )
    return jax.shard_map(
        body, mesh=mesh, in_specs=placed, out_specs=P("pool", "head"), check_vma=False
    )
```

time: 70 us -> 57.3 us (0.82)
  the two profiles are of different devices: /device:TPU:2 before, /device:TPU:65 now
where the time goes in v2:
time: 57.3 us; the launch traced here: 57.1 us
  Pallas kernels  54.2 us (95%)
  local copies, waits for them, and re-layouts  1.65 us (3%)
  between operations  1.31 us (2%)
    pallas_call x1, Pallas kernels, body(): pl.pallas_call(kernel, out_shape=jax.ShapeDtypeStruct((SUF, COLS), bf16),...  54.2 us
    pallas_call x1, local copies, waits for them, and re-layouts, body(): pl.pallas_call(kernel, out_shape=jax.ShapeDtypeStruct((SUF, COLS), bf16),...  1.65 us

profile of v2, /device:TPU:65, one launch (start us, length us, event | category | flops | bytes accessed | tf_op | source)
XLA Modules:
  0.0 57.1 jit_solution(14938611038964635337)
XLA Ops:
  1.3 54.2 %shard_map.136 = bf16[256,224]{1,0:T(8,128)(2,1)} custom-call(bf16[256,1024]{1,0:T(8,128)(2,1)} %q_nope.1, bf16[256,512]{1,0:T(8,128)(2,1)} %q_rope.1, bf16[256,512]{1,0:T(8,128)(2,1)} %new_latent.1, bf16[64,256]{1,0:T(8,128)(2,1)} %new_rope.1, bf16[1,256,512]{2,1,0:T(8,128)(2,1)} %res_latent.1, bf16[1,64,256]{2,1,0:T(8,128)(2,1)} %res_rope.1, ...), custom_call_target="tpu_custom_call" | custom-call | flops 12000000000 | bytes 14000000 | tf_op jit(solution)/shard_map/pallas_call | solution.py:418
  55.5 1.7 %copy.15 = bf16[256,224]{0,1:T(8,128)(2,1)} copy(bf16[256,224]{1,0:T(8,128)(2,1)} %shard_map.136) | data formatting | bytes 229376 | tf_op jit(solution)/shard_map/pallas_call | solution.py:418

commit v3 on v2

--- a/solution.py
+++ b/solution.py
@@ -301,24 +301,30 @@
     arrive(4, 5, 6, 7)
     arrive_core(0, 1, 2, OWN)
     expand_rest(1, 0)
-    early_heads(0, 3)
-    arrive(8, 9, 10, 11)
     expand_rest(0, 4)
-    early_heads(3, 6)
-    arrive(12, 13, 14, 15)
+    early_heads(0, 2)
+    arrive(8, 9, 10, 11, 12)
     arrive_core(4, 5, 6, 7)
     expand_rest(1, 4)
-    early_heads(6, 8)
     expand_rest(0, 8)
+    early_heads(2, 5)
+    arrive(13, 14, 15)
     arrive_core(8, 9, 10, 11)
     expand_rest(1, 8)
+    early_heads(5, 8)
     expand_rest(0, 12)
     arrive_core(12, 13, 14, 15)
     expand_rest(1, 12)
 
-    def pair(c):
+    zh = z // 2
+    groups = (
+        lax.rem(zh + 2, 4), lax.rem(zh + 1 + 2 * zp, 4), lax.rem(zh + 3 - 2 * zp, 4), zh,
+    )
+
+    def pair(c, i):
+        two = pl.ds(groups[i] * 2, 2)
         return remote(
-            share.at[c, 1], pair_in.at[c], pair_send.at[c], pair_recv.at[c], (pool, partner)
+            share.at[c, 1, two], pair_in.at[c, two], pair_send.at[c, i], pair_recv.at[c, i], (pool, partner)
         )
 
     def hop(c, i):
@@ -341,10 +347,13 @@
             add(c, of, pair_in[c, lax.rem(z + NZ + of, NZ)])
 
     def step1(c):
-        pair(c).wait_recv()
+        pair(c, 0).wait_recv()
+        pair(c, 1).wait_recv()
         paired(c, 4, 3, -3)
         for i in range(3):
             hop(c, i).start()
+        pair(c, 2).wait_recv()
+        pair(c, 3).wait_recv()
         paired(c, 1, -1)
         for i in range(3, 5):
             hop(c, i).start()
@@ -368,10 +377,9 @@
         total = share[c, 0, z].astype(f32)
         for i in range(3, 7):
             total = total + sums_in[c, i].astype(f32)
-        for g in range(4):
-            rows = lax.broadcasted_iota(jnp.int32, (PR, COLS), 0) + (c * HALF + g * PR)
-            part = jnp.where(rows < suf_len[0], total[:, g * COLS : (g + 1) * COLS], 0.0)
-            out[c * HALF + g * PR : c * HALF + (g + 1) * PR, :] = part.astype(bf16)
+        tall = jnp.concatenate([total[:, g * COLS : (g + 1) * COLS] for g in range(4)], axis=0)
+        rows = lax.broadcasted_iota(jnp.int32, (HALF, COLS), 0) + c * HALF
+        out[:, c * HALF : (c + 1) * HALF] = jnp.where(rows < suf_len[0], tall, 0.0).T.astype(bf16)
 
     for c in range(CHUNKS):
         rows = slice(c * HALF, (c + 1) * HALF)
@@ -386,13 +394,16 @@
             ld_out.wait()
         for n in range(0, DW, 512):
             po[:, n : n + 512] = dot(ho[c * HALF : (c + 1) * HALF, :], wout[:, n : n + 512]).astype(bf16)
-        for k in range(NZ):
-            for cc in range(2):
-                at = (2 * k + cc) * COLS
-                share[c, (core + cc) % 2, k] = jnp.concatenate(
-                    [po[g * PR : (g + 1) * PR, at : at + COLS] for g in range(4)], axis=1
-                )
-        pair(c).start()
+        for i in range(4):
+            g = groups[i]
+            part = po[:, pl.ds(pl.multiple_of(g * (4 * COLS), 128), 4 * COLS)]
+            for k in range(2):
+                for cc in range(2):
+                    at = (2 * k + cc) * COLS
+                    share[c, (core + cc) % 2, 2 * g + k] = jnp.concatenate(
+                        [part[n * PR : (n + 1) * PR, at : at + COLS] for n in range(4)], axis=1
+                    )
+            pair(c, i).start()
     step1(1)
     step2(0)
     step2(1)
@@ -405,7 +416,8 @@
     for o in range(16):
         over_core(o).wait_send()
     for c in range(CHUNKS):
-        pair(c).wait_send()
+        for i in range(4):
+            pair(c, i).wait_send()
         for i in range(7):
             hop(c, i).wait_send()
 
@@ -417,7 +429,7 @@
     smem = pl.BlockSpec(memory_space=pltpu.SMEM)
     return pl.pallas_call(
         kernel,
-        out_shape=jax.ShapeDtypeStruct((SUF, COLS), bf16),
+        out_shape=jax.ShapeDtypeStruct((COLS, SUF), bf16),
         in_specs=[anywhere] * 8 + [smem] * 3 + [anywhere] * 3,
         out_specs=pl.BlockSpec(memory_space=pltpu.VMEM),
         scratch_shapes=[
@@ -446,13 +458,13 @@
             vmem(CHUNKS, NZ, PR, 4 * COLS),
             vmem(CHUNKS, 7, PR, 4 * COLS),
             dma((20,)), dma((SENT,)), dma((OWN,)), dma((16,)), dma((2, 16)),
-            dma((CHUNKS,)), dma((CHUNKS,)), dma((CHUNKS, 7)), dma((CHUNKS, 7)),
+            dma((CHUNKS, 4)), dma((CHUNKS, 4)), dma((CHUNKS, 7)), dma((CHUNKS, 7)),
         ],
         compiler_params=pltpu.CompilerParams(
             collective_id=0, has_side_effects=True, vmem_limit_bytes=60 * 2**20
         ),
         cost_estimate=pl.CostEstimate(flops=12 * 10**9, bytes_accessed=14 * 10**6, transcendentals=5 * 10**6),
-    )(*args)
+    )(*args).T
 
 
 def solution(mesh):

time: 57.3 us -> 56.3 us (0.983)
  Pallas kernels: 54.2 us -> 53.2 us
    pallas_call x1 -> x0, local copies, waits for them, and re-layouts: 1.65 us -> none  [body(): pl.pallas_call(kernel, out_shape=jax.ShapeDtypeStruct((SUF, COLS), bf16),...]
    unnamed x0 -> x1, local copies, waits for them, and re-layouts: none -> 1.55 us
    pallas_call x1, Pallas kernels: 54.2 us -> 53.2 us  [body(): pl.pallas_call(kernel, out_shape=jax.ShapeDtypeStruct((COLS, SUF), bf16),...]
where the time goes in v3:
time: 56.3 us; the launch traced here: 56.1 us
  Pallas kernels  53.2 us (94%)
  local copies, waits for them, and re-layouts  1.55 us (3%)
  between operations  1.31 us (2%)
    pallas_call x1, Pallas kernels, body(): pl.pallas_call(kernel, out_shape=jax.ShapeDtypeStruct((COLS, SUF), bf16),...  53.2 us
    unnamed x1, local copies, waits for them, and re-layouts  1.55 us

profile of v3, /device:TPU:65, one launch (start us, length us, event | category | flops | bytes accessed | tf_op | source)
XLA Modules:
  0.0 56.1 jit_solution(1497618429817391810)
XLA Ops:
  1.3 53.2 %shard_map.136 = bf16[224,256]{1,0:T(8,128)(2,1)} custom-call(bf16[256,1024]{1,0:T(8,128)(2,1)} %q_nope.1, bf16[256,512]{1,0:T(8,128)(2,1)} %q_rope.1, bf16[256,512]{1,0:T(8,128)(2,1)} %new_latent.1, bf16[64,256]{1,0:T(8,128)(2,1)} %new_rope.1, bf16[1,256,512]{2,1,0:T(8,128)(2,1)} %res_latent.1, bf16[1,64,256]{2,1,0:T(8,128)(2,1)} %res_rope.1, ...), custom_call_target="tpu_custom_call" | custom-call | flops 12000000000 | bytes 14000000 | tf_op jit(solution)/shard_map/pallas_call | solution.py:430
  54.5 1.6 %copy.18 = bf16[256,224]{0,1:T(8,128)(2,1)} copy(bf16[256,224]{0,1:T(8,128)(2,1)} %bitcast.1) | data formatting | bytes 229376
